TPU v7x, 32 devices: a whole 2x2x4 slice. The times are simulated.
32 devices in a mesh: row: 8 (over z, core), col: 4 (over y, x).
Axes of the slice: x: 2, y: 2, z: 4, core: 2. Of those that a mesh axis runs over, the one named last changes fastest.
Arguments:
- loads: float32 [48, 1024, 4096], P(None, 'row', 'col'), may hold values from -6 to 6
- below_first: float32 [47, 1024, 1024], P(None, 'row', 'col'), may hold values from -0.1875 to 0.1875
- below_second: float32 [46, 1024, 1024], P(None, 'row', 'col'), may hold values from -0.1875 to 0.1875
- inverses: float32 [2, 1024, 1024], P(None, None, 'row'), may hold values from -1 to 2, as said below
Outputs:
- solved: float32 [2, 1024, 4096], P(None, None, 'col')
- remaining: float32 [46, 1024, 4096], P(None, 'row', 'col')
Inputs may be any that keep to these rules, and one draw needn't show every extreme that they name: `inverses`: each of the two matrices is lower triangular, with a diagonal from 0.5 to 2.
All inputs are finite; a program needn't handle non-finite values.
Results may differ from a plain program's by a relative error of at most 0.000084.
Values sent between devices are 32-bit elements; how exact they have to be, the bound alone decides.
A program may use at most 256 MiB of HBM per device.

v0:
```python
import jax
import jax.numpy as jnp
from jax import lax
from jax.sharding import PartitionSpec as P


def solve_block(inverse_part, block_rows):
    partial_value = jnp.dot(inverse_part, block_rows, precision=lax.Precision.HIGHEST)
    return lax.psum(partial_value, "row")


def strip_product(shard_piece, solution):
    columns = shard_piece.shape[2]
    flattened = shard_piece.reshape(-1, columns)
    return jnp.dot(flattened, solution, precision=lax.Precision.HIGHEST)


def local(loads, below_first, below_second, inverses):
    cycles, rows_dev, rhs_dev = loads.shape
    first_block = solve_block(inverses[0], loads[0])
    updated = loads[1:].reshape(-1, rhs_dev) - strip_product(
        lax.all_gather(below_first, "col", axis=2, tiled=True), first_block
    )
    updated = updated.reshape(cycles - 1, rows_dev, rhs_dev)
    second_block = solve_block(inverses[1], updated[0])
    remaining = updated[1:].reshape(-1, rhs_dev) - strip_product(
        lax.all_gather(below_second, "col", axis=2, tiled=True), second_block
    )
    solved = jnp.stack([first_block, second_block])
    return (solved, remaining.reshape(cycles - 2, rows_dev, rhs_dev))


def solution(mesh):
    in_specs = (
        P(None, "row", "col"),
        P(None, "row", "col"),
        P(None, "row", "col"),
        P(None, None, "row"),
    )
    out_specs = (P(None, None, "col"), P(None, "row", "col"))
    return jax.shard_map(local, mesh=mesh, in_specs=in_specs, out_specs=out_specs, check_vma=False)
```

profile of v0, /device:TPU:0, one launch (start us, length us, event | category | flops | bytes accessed | tf_op | source)
XLA Modules:
  0.0 741.3 jit_solution(17923245185394723700)
XLA Ops:
  8.0 0.0 all-reduce.3.cloned.1.call-start
  8.0 6.6 fusion.2
  14.7 0.0 all-reduce.3.cloned.1.call-update
  14.7 0.0 all-gather.3.cloned.1.call-start
  14.8 0.5 all-gather.3.cloned.1.call-update
  15.3 0.0 all-gather.5.cloned.1.call-start
  15.3 0.5 all-gather.5.cloned.1.call-update
  15.9 0.0 all-reduce.5.cloned.1.call-start
  15.9 19.4 %slice.22 = f32[47,128,1024]{2,1,0:T(8,128)} slice(f32[48,128,1024]{2,1,0:T(8,128)} %param.4), slice={[1:48], [0:128], [0:1024]} | slice | bytes 49283072 | tf_op jit(solution)/shard_map/slice | solution.py:21
  35.3 24.9 %copy.9 = f32[6016,1024]{0,1:T(8,128)} copy(f32[6016,1024]{1,0:T(8,128)} %bitcast.25) | data formatting | bytes 49283072 | tf_op jit(solution)/shard_map/reshape | solution.py:21
  60.3 53.8 %all-reduce.3.cloned.1.call-done = f32[1024,1024]{1,0:T(8,128)} async-done(((f32[1024,1024]{1,0:T(8,128)}), f32[1024,1024]{1,0:T(8,128)}) %all-reduce.3.cloned.1.call-update) | async-done | bytes 4194320 | tf_op jit(solution)/shard_map/psum | solution.py:9
  114.1 128.8 %all-gather.3.cloned.1.call-done = f32[47,128,1024]{2,1,0:T(8,128)} async-done(((f32[47,128,256]{2,1,0:T(8,128)}), f32[47,128,1024]{2,1,0:T(8,128)}) %all-gather.3.cloned.1.call-update) | async-done | bytes 24641552 | tf_op jit(solution)/shard_map/all_gather | solution.py:22
  242.8 0.0 copy-start
  242.8 178.1 %bitcast_subtract_fusion = f32[6016,1024]{0,1:T(8,128)} fusion(f32[6016,1024]{0,1:T(8,128)} %copy.9, f32[1024,1024]{1,0:T(8,128)} %all-reduce.3.cloned.1.call-done, f32[6016,1024]{1,0:T(8,128)} %bitcast.29), kind=kOutput, calls=%fused_computation | convolution fusion | flops 75704958976 | bytes 78118912 | tf_op jit(solution)/shard_map/dot_general | solution.py:15
  421.0 0.0 copy-done
  421.0 6.0 convolution_bitcast_fusion
  427.0 0.0 all-reduce.5.cloned.1.call-update
  427.0 36.3 %all-gather.5.cloned.1.call-done = f32[46,128,1024]{2,1,0:T(8,128)} async-done(((f32[46,128,256]{2,1,0:T(8,128)}), f32[46,128,1024]{2,1,0:T(8,128)}) %all-gather.5.cloned.1.call-update) | async-done | bytes 24117264 | tf_op jit(solution)/shard_map/all_gather | solution.py:27
  463.4 60.8 %all-reduce.5.cloned.1.call-done = f32[1024,1024]{1,0:T(8,128)} async-done(((f32[1024,1024]{1,0:T(8,128)}), f32[1024,1024]{1,0:T(8,128)}) %all-reduce.5.cloned.1.call-update) | async-done | bytes 4194320 | tf_op jit(solution)/shard_map/psum | solution.py:9
  524.1 176.9 %slice_subtract_fusion = f32[5888,1024]{0,1:T(8,128)} fusion(f32[6016,1024]{0,1:T(8,128)} %bitcast_subtract_fusion, f32[1024,1024]{1,0:T(8,128)} %all-reduce.5.cloned.1.call-done, f32[5888,1024]{1,0:T(8,128)} %bitcast.30), kind=kOutput, calls=%fused_computation.1 | convolution fusion | flops 74094215168 | bytes 76546048 | tf_op jit(solution)/shard_map/dot_general | solution.py:15
  701.0 24.1 %copy.11 = f32[5888,1024]{1,0:T(8,128)} copy(f32[5888,1024]{0,1:T(8,128)} %slice_subtract_fusion) | data formatting | bytes 48234496 | tf_op jit(solution)/shard_map/sub | solution.py:26
  725.1 8.5 %pad_maximum_fusion = f32[2,1024,1024]{2,1,0:T(8,128)} fusion(f32[1,1024,1024]{2,1,0:T(8,128)} %bitcast.28, f32[1,1024,1024]{2,1,0:T(8,128)} %bitcast.27), kind=kLoop, calls=%fused_computation.2 | loop fusion | flops 2097152 | bytes 16777216 | tf_op jit(solution)/shard_map/stack | solution.py:29
Async XLA Ops:
  8.0 106.1 %all-reduce.3.cloned.1.call-start = ((), (), s32[]{:S(2)}) async-start(), calls=%async_computation | async-start | bytes 8388608 | tf_op jit(solution)/shard_map/psum | solution.py:9
  14.7 228.1 %all-gather.3.cloned.1.call-start = ((), (), s32[]{:S(2)}) async-start(), calls=%async_computation.1 | async-start | bytes 30801920 | tf_op jit(solution)/shard_map/all_gather | solution.py:22
  15.3 448.1 %all-gather.5.cloned.1.call-start = ((), (), s32[]{:S(2)}) async-start(), calls=%async_computation.3 | async-start | bytes 30146560 | tf_op jit(solution)/shard_map/all_gather | solution.py:27
  15.9 508.3 %all-reduce.5.cloned.1.call-start = ((), (), s32[]{:S(2)}) async-start(), calls=%async_computation.2 | async-start | bytes 8388608 | tf_op jit(solution)/shard_map/psum | solution.py:9
  242.8 178.1 %copy-start = (f32[2,1024,128]{2,1,0:T(8,128)S(1)}, f32[2,1024,128]{2,1,0:T(8,128)}, u32[]{:S(2)}) copy-start(f32[2,1024,128]{2,1,0:T(8,128)} %param.7) | copy-start | bytes 3145732
Sparse Core Ops, SparseCore 0:
  14.8 99.2 all-reduce.2
  427.1 96.9 all-reduce.4
Sparse Core Ops, SparseCore 1:
  17.0 225.8 all-gather.2
  244.6 218.7 all-gather.4
where the time goes:
time: 746 us; the launch traced here: 741 us
  matrix products  368 us (49%)
  waiting for transfers between devices  281 us (38%)
  local copies, waits for them, and re-layouts  68.4 us (9%)
  between operations  15.7 us (2%)
  other arithmetic  8.53 us (1%)
    dot_general x2, matrix products, strip_product(): return jnp.dot(flattened, solution, precision=lax.Precision.HIGHEST)  355 us
    all_gather x1, waiting for transfers between devices, local(): lax.all_gather(below_first, 'col', axis=2, tiled=True)  129 us
    psum x2, waiting for transfers between devices, solve_block(): return lax.psum(partial_value, 'row')  115 us
    all_gather x1, waiting for transfers between devices, local(): lax.all_gather(below_second, 'col', axis=2, tiled=True)  36.3 us
    reshape x1, local copies, waits for them, and re-layouts, local(): loads[1:].reshape(-1, rhs_dev)  24.9 us
    sub x1, local copies, waits for them, and re-layouts, local(): updated[1:].reshape(-1, rhs_dev)  24.1 us
    slice x1, local copies, waits for them, and re-layouts, local(): loads[1:].reshape(-1, rhs_dev)  19.4 us
  transfers between devices with their start and end apart: 4, of which 4 were waited for; matrix products, arithmetic and copies ran while one was open for 31% of the time, Pallas kernels for 0%

commit v1 on v0

--- a/solution.py
+++ b/solution.py
@@ -16,11 +16,26 @@
 
 
 def local(loads, below_first, below_second, inverses):
+
+    def _lay_node(xin):
+        across = "col"
+        p_count = jax.lax.axis_size(across)
+        items = list(map(lambda at: (at, (at + 1) % p_count), range(p_count)))
+        frames = list(map(lambda at: (at, (at - 1) % p_count), range(p_count)))
+        later, o_now = ([xin], [xin])
+        for _ in range(p_count // 2):
+            later.append(jax.lax.ppermute(later[-1], across, items))
+        for _ in range((p_count - 1) // 2):
+            o_now.append(jax.lax.ppermute(o_now[-1], across, frames))
+        return jnp.roll(
+            jnp.concatenate([*later[::-1], *o_now[1:]], axis=2),
+            shift=(jax.lax.axis_index(across) - p_count // 2) * xin.shape[2],
+            axis=2,
+        )
+
     cycles, rows_dev, rhs_dev = loads.shape
     first_block = solve_block(inverses[0], loads[0])
-    updated = loads[1:].reshape(-1, rhs_dev) - strip_product(
-        lax.all_gather(below_first, "col", axis=2, tiled=True), first_block
-    )
+    updated = loads[1:].reshape(-1, rhs_dev) - strip_product(_lay_node(below_first), first_block)
     updated = updated.reshape(cycles - 1, rows_dev, rhs_dev)
     second_block = solve_block(inverses[1], updated[0])
     remaining = updated[1:].reshape(-1, rhs_dev) - strip_product(

time: 746 us -> 867 us (1.16)
  waiting for transfers between devices: 281 us -> 570 us
  matrix products: 368 us -> 180 us
  local copies, waits for them, and re-layouts: 68.4 us -> 86.4 us
    ppermute x0 -> x3, waiting for transfers between devices: none -> 358 us  [the longest x2 244 us: _lay_node(): later.append(jax.lax.ppermute(later[-1], across, items))]
    dot_general x2, matrix products: 355 us -> 169 us  [strip_product(): return jnp.dot(flattened, solution, precision=lax.Precision.HIGHEST)]
    all_gather x1 -> x0, waiting for transfers between devices: 129 us -> none  [local(): lax.all_gather(below_first, 'col', axis=2, tiled=True)]
    all_gather x1, waiting for transfers between devices: 36.3 us -> 116 us  [local(): lax.all_gather(below_second, 'col', axis=2, tiled=True)]
    unnamed x2 -> x15, local copies, waits for them, and re-layouts: 0.01 us -> 45.1 us
    reshape x1 -> x0, local copies, waits for them, and re-layouts: 24.9 us -> none  [local(): loads[1:].reshape(-1, rhs_dev)]
    sub x1 -> x0, local copies, waits for them, and re-layouts: 24.1 us -> none  [local(): updated[1:].reshape(-1, rhs_dev)]
    psum x2, waiting for transfers between devices: 115 us -> 95.5 us  [solve_block(): return lax.psum(partial_value, 'row')]
  transfers between devices with their start and end apart: 4 -> 6, of which waited for: 4 -> 5; matrix products, arithmetic and copies ran while one was open for 31% -> 11% of each run, Pallas kernels for 0% -> 0%
where the time goes in v1:
time: 867 us
  waiting for transfers between devices  570 us (66%)
  matrix products  180 us (21%)
  local copies, waits for them, and re-layouts  86.4 us (10%)
  between operations  15.5 us (2%)
  other arithmetic  8.86 us (1%)
    ppermute x2, waiting for transfers between devices, _lay_node(): later.append(jax.lax.ppermute(later[-1], across, items))  244 us
    dot_general x2, matrix products, strip_product(): return jnp.dot(flattened, solution, precision=lax.Precision.HIGHEST)  169 us
    all_gather x1, waiting for transfers between devices, local(): lax.all_gather(below_second, 'col', axis=2, tiled=True)  116 us
    ppermute x1, waiting for transfers between devices, _lay_node(): o_now.append(jax.lax.ppermute(o_now[-1], across, frames))  115 us
    psum x2, waiting for transfers between devices, solve_block(): return lax.psum(partial_value, 'row')  95.5 us
    unnamed x15, local copies, waits for them, and re-layouts  45.1 us
    slice x1, local copies, waits for them, and re-layouts, local(): loads[1:].reshape(-1, rhs_dev)  17.6 us
    dynamic_slice x1, local copies, waits for them, and re-layouts, _lay_node(): jnp.roll(jnp.concatenate([*later[::-1], *o_now[1:]], axis=2), shift=(jax....  17.6 us
  transfers between devices with their start and end apart: 6, of which 5 were waited for; matrix products, arithmetic and copies ran while one was open for 11% of the time, Pallas kernels for 0%

profile of v1, /device:TPU:0, one launch (start us, length us, event | category | flops | bytes accessed | tf_op | source)
XLA Modules:
  0.0 866.9 jit_solution(7101745965652469120)
XLA Ops:
  8.0 0.0 all-reduce.3.cloned.1.call-start
  8.0 3.0 collective-permute-start
  11.0 134.0 %collective-permute-done = f32[47,128,256]{2,1,0:T(8,128)} collective-permute-done((f32[47,128,256]{2,1,0:T(8,128)}, f32[47,128,256]{2,1,0:T(8,128)}, u32[]{:S(2)}, u32[]{:S(2)}) %collective-permute-start) | collective-permute-done | bytes 6160416 | tf_op jit(solution)/shard_map/ppermute | solution.py:27
  145.0 0.8 collective-permute-start.1
  145.8 2.1 collective-permute-start.2
  147.9 6.6 fusion.2
  154.6 0.0 all-reduce.3.cloned.1.call-update
  154.6 0.0 all-reduce.5.cloned.1.call-start
  154.7 17.6 %slice.22 = f32[47,128,1024]{2,1,0:T(8,128)} slice(f32[48,128,1024]{2,1,0:T(8,128)} %param.4), slice={[1:48], [0:128], [0:1024]} | slice | bytes 49283072 | tf_op jit(solution)/shard_map/slice | solution.py:38
  172.3 109.6 %collective-permute-done.1 = f32[47,128,256]{2,1,0:T(8,128)} collective-permute-done((f32[47,128,256]{2,1,0:T(8,128)}, f32[47,128,256]{2,1,0:T(8,128)}, u32[]{:S(2)}, u32[]{:S(2)}) %collective-permute-start.1) | collective-permute-done | bytes 6160416 | tf_op jit(solution)/shard_map/ppermute | solution.py:27
  281.9 6.1 constant_dynamic-update-slice_fusion.7
  288.0 6.2 constant_dynamic-update-slice_fusion.6
  294.2 0.0 slice-done.1
  294.2 3.1 constant_dynamic-update-slice_fusion.5
  297.3 114.7 %collective-permute-done.2 = f32[47,128,256]{2,1,0:T(8,128)} collective-permute-done((f32[47,128,256]{2,1,0:T(8,128)}, f32[47,128,256]{2,1,0:T(8,128)}, u32[]{:S(2)}, u32[]{:S(2)}) %collective-permute-start.2) | collective-permute-done | bytes 6160416 | tf_op jit(solution)/shard_map/ppermute | solution.py:29
  412.1 6.1 constant_dynamic-update-slice_fusion.4
  418.2 6.1 constant_dynamic-update-slice_fusion.3
  424.3 6.1 constant_dynamic-update-slice_fusion.2
  430.4 3.2 constant_dynamic-update-slice_fusion.1
  433.6 6.1 constant_dynamic-update-slice_fusion
  439.7 17.6 %constant_dynamic-slice_fusion = f32[47,128,1024]{2,1,0:T(8,128)} fusion(f32[47,128,2048]{2,1,0:T(8,128)} %constant_dynamic-update-slice_fusion, s32[]{:T(128)S(6)} %select_n.14), kind=kLoop, calls=%fused_computation.20 | loop fusion | bytes 49283076 | tf_op jit(solution)/shard_map/jit(_roll_dynamic)/dynamic_slice | solution.py:30
  457.3 84.0 %bitcast_subtract_fusion = f32[6016,1024]{1,0:T(8,128)S(1)} fusion(f32[47,128,1024]{2,1,0:T(8,128)} %slice.22, f32[6016,1024]{1,0:T(8,128)} %bitcast.24, f32[1024,1024]{1,0:T(8,128)} %all-reduce.3.cloned.1.call-done), kind=kOutput, calls=%fused_computation | convolution fusion | flops 75704958976 | bytes 78118912 | tf_op jit(solution)/shard_map/dot_general | solution.py:15
  541.3 8.1 copy-done.1
  549.5 0.0 copy-done
  549.5 5.0 convolution_bitcast_fusion
  554.4 0.0 all-reduce.5.cloned.1.call-update
  554.4 0.0 all-gather.2.cloned.1.call-start
  554.5 0.5 all-gather.2.cloned.1.call-update
  555.0 95.5 %all-reduce.5.cloned.1.call-done = f32[1024,1024]{1,0:T(8,128)} async-done(((f32[1024,1024]{1,0:T(8,128)}), f32[1024,1024]{1,0:T(8,128)}) %all-reduce.5.cloned.1.call-update) | async-done | bytes 4194320 | tf_op jit(solution)/shard_map/psum | solution.py:9
  650.5 8.9 %pad_maximum_fusion = f32[2,1024,1024]{2,1,0:T(8,128)} fusion(f32[1,1024,1024]{2,1,0:T(8,128)} %bitcast.28, f32[1,1024,1024]{2,1,0:T(8,128)} %bitcast.27), kind=kLoop, calls=%fused_computation.2 | loop fusion | flops 2097152 | bytes 16777216 | tf_op jit(solution)/shard_map/stack | solution.py:44
  659.4 115.6 %all-gather.2.cloned.1.call-done = f32[46,128,1024]{2,1,0:T(8,128)} async-done(((f32[46,128,256]{2,1,0:T(8,128)}), f32[46,128,1024]{2,1,0:T(8,128)}) %all-gather.2.cloned.1.call-update) | async-done | bytes 24117264 | tf_op jit(solution)/shard_map/all_gather | solution.py:42
  775.0 84.5 %slice_subtract_fusion = f32[5888,1024]{1,0:T(8,128)} fusion(f32[6016,1024]{1,0:T(8,128)} %copy-done.1, f32[1024,1024]{1,0:T(8,128)} %all-reduce.5.cloned.1.call-done, f32[5888,1024]{1,0:T(8,128)} %bitcast.29), kind=kOutput, calls=%fused_computation.1 | convolution fusion | flops 74094215168 | bytes 76546048 | tf_op jit(solution)/shard_map/dot_general | solution.py:15
  (7 shorter events, 0.0 us)
Async XLA Ops:
  8.0 449.3 %all-reduce.3.cloned.1.call-start = ((), (), s32[]{:S(2)}) async-start(), calls=%async_computation | async-start | bytes 8388608 | tf_op jit(solution)/shard_map/psum | solution.py:9
  8.0 137.0 %collective-permute-start = (f32[47,128,256]{2,1,0:T(8,128)}, f32[47,128,256]{2,1,0:T(8,128)}, u32[]{:S(2)}, u32[]{:S(2)}) collective-permute-start(f32[47,128,256]{2,1,0:T(8,128)} %param.5), channel_id=1, source_target_pairs={{0,1},{1,2},{2,3},{3,0},{4,5},{5,6},{6,7},{7,4},{8,9},{9,10},{10,1... | collective-permute-start | bytes 18481160 | tf_op jit(solution)/shard_map/ppermute | solution.py:27
  145.0 136.9 %collective-permute-start.1 = (f32[47,128,256]{2,1,0:T(8,128)}, f32[47,128,256]{2,1,0:T(8,128)}, u32[]{:S(2)}, u32[]{:S(2)}) collective-permute-start(f32[47,128,256]{2,1,0:T(8,128)} %collective-permute-done), channel_id=1, source_target_pairs={{0,1},{1,2},{2,3},{3,0},{4,5},{5,6},{6,7},{7,4},{8,9},{9,10},{10,1... | collective-permute-start | bytes 18481160 | tf_op jit(solution)/shard_map/ppermute | solution.py:27
  145.8 266.3 %collective-permute-start.2 = (f32[47,128,256]{2,1,0:T(8,128)}, f32[47,128,256]{2,1,0:T(8,128)}, u32[]{:S(2)}, u32[]{:S(2)}) collective-permute-start(f32[47,128,256]{2,1,0:T(8,128)} %param.5), channel_id=1, source_target_pairs={{0,3},{1,0},{2,1},{3,2},{4,7},{5,4},{6,5},{7,6},{8,11},{9,8},{10,9... | collective-permute-start | bytes 18481160 | tf_op jit(solution)/shard_map/ppermute | solution.py:29
  154.6 495.9 %all-reduce.5.cloned.1.call-start = ((), (), s32[]{:S(2)}) async-start(), calls=%async_computation.1 | async-start | bytes 8388608 | tf_op jit(solution)/shard_map/psum | solution.py:9
  172.3 121.9 %slice-start = ((s8[6160384]{0:T(1024)(128)(4,1)}), s8[1966080]{0:T(1024)(128)(4,1)S(1)}, s32[]{:S(2)}) async-start(s8[6160384]{0:T(1024)(128)(4,1)} %bitcast.25), calls=%async_computation.3 | async-start | bytes 3932160
  172.3 121.9 %slice-start.1 = ((s8[6160384]{0:T(1024)(128)(4,1)}), s8[4194304]{0:T(1024)(128)(4,1)S(1)}, s32[]{:S(2)}) async-start(s8[6160384]{0:T(1024)(128)(4,1)} %bitcast.25), calls=%async_computation.4 | async-start | bytes 8388608
  457.3 92.2 %copy-start = (f32[2,1024,128]{2,1,0:T(8,128)S(1)}, f32[2,1024,128]{2,1,0:T(8,128)}, u32[]{:S(2)}) copy-start(f32[2,1024,128]{2,1,0:T(8,128)} %param.7) | copy-start | bytes 3145732
  541.3 8.1 copy-start.1
  554.4 220.5 %all-gather.2.cloned.1.call-start = ((), (), s32[]{:S(2)}) async-start(), calls=%async_computation.2 | async-start | bytes 30146560 | tf_op jit(solution)/shard_map/all_gather | solution.py:42
Sparse Core Ops, SparseCore 0:
  154.7 97.0 all-reduce.2
  554.5 95.9 all-reduce.4
Sparse Core Ops, SparseCore 1:
  556.8 218.1 all-gather.1

commit v2 on v0

--- a/solution.py
+++ b/solution.py
@@ -5,8 +5,12 @@
 
 
 def solve_block(inverse_part, block_rows):
+
+    def node_prepare(mine, comm_axis):
+        return lax.all_gather(mine, comm_axis).sum(axis=0)
+
     partial_value = jnp.dot(inverse_part, block_rows, precision=lax.Precision.HIGHEST)
-    return lax.psum(partial_value, "row")
+    return node_prepare(partial_value, "row")
 
 
 def strip_product(shard_piece, solution):

time: 746 us -> 1340 us (1.80)
  waiting for transfers between devices: 281 us -> 907 us
  matrix products: 368 us -> 261 us
  local copies, waits for them, and re-layouts: 68.4 us -> 109 us
  other arithmetic: 8.53 us -> 39.1 us
    all_gather x0 -> x2, waiting for transfers between devices: none -> 534 us  [node_prepare(): return lax.all_gather(mine, comm_axis).sum(axis=0)]
    all_gather x1, waiting for transfers between devices: 36.3 us -> 166 us  [local(): lax.all_gather(below_second, 'col', axis=2, tiled=True)]
    psum x2 -> x0, waiting for transfers between devices: 115 us -> none  [solve_block(): return lax.psum(partial_value, 'row')]
    dot_general x2, matrix products: 355 us -> 249 us  [strip_product(): return jnp.dot(flattened, solution, precision=lax.Precision.HIGHEST)]
    all_gather x1, waiting for transfers between devices: 129 us -> 205 us  [local(): lax.all_gather(below_first, 'col', axis=2, tiled=True)]
    unnamed x2 -> x3, local copies, waits for them, and re-layouts: 0.01 us -> 34.9 us
    reduce_sum x0 -> x2, other arithmetic: none -> 30.6 us  [node_prepare(): return lax.all_gather(mine, comm_axis).sum(axis=0)]
  transfers between devices with their start and end apart: 4 -> 4, of which waited for: 4 -> 4; matrix products, arithmetic and copies ran while one was open for 31% -> 9% of each run, Pallas kernels for 0% -> 0%
where the time goes in v2:
time: 1340 us; the launch traced here: 1330 us
  waiting for transfers between devices  907 us (68%)
  matrix products  261 us (19%)
  local copies, waits for them, and re-layouts  109 us (8%)
  other arithmetic  39.1 us (3%)
  between operations  14 us (1%)
    all_gather x2, waiting for transfers between devices, node_prepare(): return lax.all_gather(mine, comm_axis).sum(axis=0)  534 us
    dot_general x2, matrix products, strip_product(): return jnp.dot(flattened, solution, precision=lax.Precision.HIGHEST)  249 us
    all_gather x1, waiting for transfers between devices, local(): lax.all_gather(below_first, 'col', axis=2, tiled=True)  205 us
    all_gather x1, waiting for transfers between devices, local(): lax.all_gather(below_second, 'col', axis=2, tiled=True)  166 us
    unnamed x3, local copies, waits for them, and re-layouts  34.9 us
    reduce_sum x2, other arithmetic, node_prepare(): return lax.all_gather(mine, comm_axis).sum(axis=0)  30.6 us
  transfers between devices with their start and end apart: 4, of which 4 were waited for; matrix products, arithmetic and copies ran while one was open for 9% of the time, Pallas kernels for 0%

profile of v2, /device:TPU:0, one launch (start us, length us, event | category | flops | bytes accessed | tf_op | source)
XLA Modules:
  0.0 1330.6 jit_solution(4640615532271035752)
XLA Ops:
  7.2 0.0 all-gather.11.cloned.1.call-start
  7.2 6.6 fusion.2
  13.8 0.0 all-gather.11.cloned.1.call-update
  13.9 0.0 all-gather.7.cloned.1.call-start
  13.9 0.7 all-gather.7.cloned.1.call-update
  14.6 0.0 all-gather.13.cloned.1.call-start
  14.7 19.3 %slice.22 = f32[47,128,1024]{2,1,0:T(8,128)} slice(f32[48,128,1024]{2,1,0:T(8,128)} %param.4), slice={[1:48], [0:128], [0:1024]} | slice | bytes 49283072 | tf_op jit(solution)/shard_map/slice | solution.py:25
  33.9 25.2 %copy.13 = f32[6016,1024]{0,1:T(8,128)} copy(f32[6016,1024]{1,0:T(8,128)} %bitcast.31) | data formatting | bytes 49283072 | tf_op jit(solution)/shard_map/reshape | solution.py:25
  59.1 246.2 %all-gather.11.cloned.1.call-done = f32[8192,1024]{1,0:T(8,128)} async-done(((f32[1024,1024]{1,0:T(8,128)}), f32[8192,1024]{1,0:T(8,128)}) %all-gather.11.cloned.1.call-update) | async-done | bytes 33554448 | tf_op jit(solution)/shard_map/all_gather | solution.py:10
  305.4 18.0 %reduce_sum.18 = f32[1024,1024]{1,0:T(8,128)} reduce(f32[8,1024,1024]{2,1,0:T(8,128)} %bitcast.32, f32[]{:T(128)} %constant.0.clone.1), dimensions={0}, to_apply=%region_0.0 | reduce | flops 7340032 | bytes 37748740 | tf_op jit(solution)/shard_map/reduce_sum | solution.py:10
  323.3 205.4 %all-gather.7.cloned.1.call-done = f32[47,128,1024]{2,1,0:T(8,128)} async-done(((f32[47,128,256]{2,1,0:T(8,128)}), f32[47,128,1024]{2,1,0:T(8,128)}) %all-gather.7.cloned.1.call-update) | async-done | bytes 24641552 | tf_op jit(solution)/shard_map/all_gather | solution.py:26
  528.7 0.0 copy-start
  528.7 163.4 %bitcast_subtract_fusion = f32[6016,1024]{0,1:T(8,128)} fusion(f32[6016,1024]{0,1:T(8,128)} %copy.13, f32[1024,1024]{1,0:T(8,128)} %reduce_sum.18, f32[6016,1024]{1,0:T(8,128)} %bitcast.37), kind=kOutput, calls=%fused_computation.1 | convolution fusion | flops 75704958976 | bytes 78118912 | tf_op jit(solution)/shard_map/dot_general | solution.py:19
  692.1 0.0 copy-done
  692.1 6.0 convolution_bitcast_fusion
  698.1 0.0 all-gather.13.cloned.1.call-update
  698.1 0.0 all-gather.9.cloned.1.call-start
  698.2 0.5 all-gather.9.cloned.1.call-update
  698.7 288.2 %all-gather.13.cloned.1.call-done = f32[8192,1024]{0,1:T(8,128)} async-done(((f32[1024,1024]{0,1:T(8,128)}), f32[8192,1024]{0,1:T(8,128)}) %all-gather.13.cloned.1.call-update) | async-done | bytes 33554448 | tf_op jit(solution)/shard_map/all_gather | solution.py:10
  986.9 34.9 %copy.16 = f32[128,8,8,1024]{3,2,1,0:T(8,128)S(1)} copy(f32[128,8,8,1024]{3,1,2,0:T(8,128)} %bitcast.33) | data formatting | bytes 67108864
  1021.8 12.6 bitcast_reduce_fusion
  1034.5 5.4 copy.14
  1039.8 166.0 %all-gather.9.cloned.1.call-done = f32[46,128,1024]{2,1,0:T(8,128)} async-done(((f32[46,128,256]{2,1,0:T(8,128)}), f32[46,128,1024]{2,1,0:T(8,128)}) %all-gather.9.cloned.1.call-update) | async-done | bytes 24117264 | tf_op jit(solution)/shard_map/all_gather | solution.py:31
  1205.8 85.5 %slice_subtract_fusion = f32[5888,1024]{0,1:T(8,128)} fusion(f32[6016,1024]{0,1:T(8,128)} %bitcast_subtract_fusion, f32[1024,1024]{0,1:T(8,128)} %bitcast_reduce_fusion, f32[5888,1024]{1,0:T(8,128)} %bitcast.38), kind=kOutput, calls=%fused_computation.2 | convolution fusion | flops 74094215168 | bytes 76546048 | tf_op jit(solution)/shard_map/dot_general | solution.py:19
  1291.2 24.1 %copy.15 = f32[5888,1024]{1,0:T(8,128)} copy(f32[5888,1024]{0,1:T(8,128)} %slice_subtract_fusion) | data formatting | bytes 48234496 | tf_op jit(solution)/shard_map/sub | solution.py:30
  1315.3 8.5 pad_maximum_fusion
Async XLA Ops:
  7.2 298.2 %all-gather.11.cloned.1.call-start = ((), (), s32[]{:S(2)}) async-start(), calls=%async_computation.2 | async-start | bytes 37748736 | tf_op jit(solution)/shard_map/all_gather | solution.py:10
  13.9 514.8 %all-gather.7.cloned.1.call-start = ((), (), s32[]{:S(2)}) async-start(), calls=%async_computation | async-start | bytes 30801920 | tf_op jit(solution)/shard_map/all_gather | solution.py:26
  14.6 972.3 %all-gather.13.cloned.1.call-start = ((), (), s32[]{:S(2)}) async-start(), calls=%async_computation.3 | async-start | bytes 37748736 | tf_op jit(solution)/shard_map/all_gather | solution.py:10
  528.7 163.4 %copy-start = (f32[2,1024,128]{2,1,0:T(8,128)S(1)}, f32[2,1024,128]{2,1,0:T(8,128)}, u32[]{:S(2)}) copy-start(f32[2,1024,128]{2,1,0:T(8,128)} %param.7) | copy-start | bytes 3145732
  698.1 507.7 %all-gather.9.cloned.1.call-start = ((), (), s32[]{:S(2)}) async-start(), calls=%async_computation.1 | async-start | bytes 30146560 | tf_op jit(solution)/shard_map/all_gather | solution.py:31
Sparse Core Ops, SparseCore 0:
  14.0 291.3 all-gather.10
  307.2 221.4 all-gather.6
  698.2 288.6 all-gather.12
  988.6 217.1 all-gather.8
